TPU v7x, 32 devices: a whole 2x2x4 slice. The times are simulated.
32 devices in a mesh: seqin: 4 (over y, x), seqout: 2 (over core), head: 4 (over z).
Axes of the slice: x: 2, y: 2, z: 4, core: 2. Of those that a mesh axis runs over, the one named last changes fastest.
Arguments:
- queries: bfloat16 [8192, 4096], P(('seqin', 'seqout'), 'head'), may hold values from -6 to 6
- keys: bfloat16 [8192, 4096], P(('seqin', 'seqout'), 'head'), may hold values from -6 to 6
- values: bfloat16 [8192, 4096], P(('seqin', 'seqout'), 'head'), may hold values from -120 to 120
- gain: float32 [4096], P('head'), may hold values from 0.5 to 1.5
- cotangent: bfloat16 [8192, 4096], P(('seqin', 'seqout'), 'head'), may hold values from -6 to 6
Outputs:
- mixed: bfloat16 [8192, 4096], P(('seqin', 'seqout'), 'head')
- grad_queries: bfloat16 [8192, 4096], P(('seqin', 'seqout'), 'head')
- grad_keys: bfloat16 [8192, 4096], P(('seqin', 'seqout'), 'head')
- grad_values: bfloat16 [8192, 4096], P(('seqin', 'seqout'), 'head')
All inputs are finite; a program needn't handle non-finite values.
Results may differ from a plain program's by a relative error of at most 0.0089.
Values sent between devices are 32-bit elements; how exact they have to be, the bound alone decides.
A program may use at most 192 MiB of HBM per device.

v0:
```python
import functools

import jax
import jax.numpy as jnp
from jax import lax
from jax.experimental import pallas as pl
from jax.experimental.pallas import tpu as pltpu
from jax.sharding import PartitionSpec as P

E = 128
BLOCK = 512
NORM = E
PAY = E + 8
F32 = jnp.float32
BF16 = jnp.bfloat16
MESH = pl.DeviceIdType.MESH


def features(x):
    xf = x.astype(F32)
    return jnp.where(xf > 0, xf + 1.0, jnp.exp(jnp.minimum(xf, 0.0))).astype(BF16)


def slope(x):
    return jnp.exp(jnp.minimum(x.astype(F32), 0.0))


def dot(a, b, ca=1, cb=0):
    return lax.dot_general(a, b, (((ca,), (cb,)), ((), ())), preferred_element_type=F32)


def split(x):
    hi = x.astype(BF16)
    return hi, (x - hi.astype(F32)).astype(BF16)


def kernel(dims, q_hbm, k_hbm, v_hbm, gain_ref, c_hbm, mixed_hbm, gq_hbm, gk_hbm, gv_hbm,
           qv, kv, vv, cv, fq, fk, wts, att, den, gn, dvp, om, oq, ok, ov,
           kvb, rvb, sh, tot, r0, tx, rx, fin, pfx, stat, stat_in, scl,
           in_sem, out_sem, s0, q0, sx, rxs, s2, q2, ss, rs):
    heads, nblk, block, n_in, n_out, n_head, width = dims
    half = heads // 2
    tile = block // 2
    n_seq = n_in * n_out
    nchips = n_seq // 2
    stages = nchips.bit_length() - 1
    a_in, a_out, a_head = lax.axis_index("seqin"), lax.axis_index("seqout"), lax.axis_index("head")
    me = a_in * n_out + a_out
    core = lax.rem(me, 2)
    mine = core * half
    theirs = (1 - core) * half

    def bit(m):
        return lax.rem(lax.div(me, m), 2)

    def peer(m):
        other = me + m - 2 * m * bit(m)
        return (lax.div(other, n_out), lax.rem(other, n_out), a_head)

    def zpeer(d):
        return (a_in, a_out, lax.rem(a_head + d, n_head))

    def fetch(array, h):
        src, dst = ((k_hbm, kv), (v_hbm, vv), (q_hbm, qv), (c_hbm, cv))[array]
        cols = pl.ds(pl.multiple_of(h * E, E), E)
        return pltpu.make_async_copy(src.at[:, cols], dst.at[h], in_sem.at[array, h])

    def put(array, h):
        src, dst = ((om, mixed_hbm), (oq, gq_hbm), (ok, gk_hbm), (ov, gv_hbm))[array]
        cols = pl.ds(pl.multiple_of(h * E, E), E)
        return pltpu.make_async_copy(src.at[h], dst.at[:, cols], out_sem.at[array, h])

    def each(n, body):
        def step(j, carry):
            body(j)
            return carry
        lax.fori_loop(0, n, step, 0)

    def order(j):
        return lax.rem(theirs + j, heads)

    def start_kv(j):
        fetch(0, order(j)).start()
        fetch(1, order(j)).start()

    def start_qc(h):
        fetch(2, h).start()
        fetch(3, h).start()

    each(heads, start_kv)
    each(heads, start_qc)

    barrier = pltpu.get_barrier_semaphore()
    masks = [1 << s for s in range(stages + 1)]
    for m in masks:
        pl.semaphore_signal(barrier, inc=1, device_id=peer(m), device_id_type=MESH)
    for d in range(1, n_head):
        pl.semaphore_signal(barrier, inc=1, device_id=zpeer(d), device_id_type=MESH)

    def swap(dirn, j):
        return pltpu.make_async_remote_copy(
            src_ref=tot.at[dirn, theirs + j], dst_ref=r0.at[dirn, j],
            send_sem=s0.at[dirn, j], recv_sem=q0.at[dirn, j],
            device_id=peer(1), device_id_type=MESH)

    def hop(dirn, s, j):
        return pltpu.make_async_remote_copy(
            src_ref=tx.at[dirn, s, j], dst_ref=rx.at[dirn, s, j],
            send_sem=sx.at[dirn, s, j], recv_sem=rxs.at[dirn, s, j],
            device_id=peer(2 << s), device_id_type=MESH)

    def back(dirn, j):
        return pltpu.make_async_remote_copy(
            src_ref=fin.at[dirn, j], dst_ref=pfx.at[dirn, mine + j],
            send_sem=s2.at[dirn, j], recv_sem=q2.at[dirn, j],
            device_id=peer(1), device_id_type=MESH)

    def back_in(dirn, j):
        return pltpu.make_async_remote_copy(
            src_ref=fin.at[dirn, j], dst_ref=pfx.at[dirn, theirs + j],
            send_sem=s2.at[dirn, j], recv_sem=q2.at[dirn, j],
            device_id=peer(1), device_id_type=MESH)

    def chip_total(dirn):
        def body(j):
            swap(dirn, j).wait_recv()
            tx[dirn, 0, j] = tot[dirn, mine + j] + r0[dirn, j]
            hop(dirn, 0, j).start()
        each(half, body)

    def hop_on(dirn, s):
        def body(j):
            hop(dirn, s, j).wait_recv()
            if s + 1 < stages:
                tx[dirn, s + 1, j] = tx[dirn, s, j] + rx[dirn, s, j]
                hop(dirn, s + 1, j).start()
                return
            total = jnp.zeros((PAY, E), F32)
            for i in range(stages):
                before = bit(2 << i) == 1 - dirn
                total = total + jnp.where(before, rx[dirn, i, j], 0.0)
            near = core == dirn
            own, other = tot[dirn, mine + j], r0[dirn, j]
            fin[dirn, j] = total + jnp.where(near, own, 0.0)
            pfx[dirn, mine + j] = total + jnp.where(near, 0.0, other)
            back(dirn, j).start()
        each(half, body)

    def arrive(dirn):
        each(half, lambda j: back_in(dirn, j).wait_recv())

    def drain(dirn):
        def body(j):
            swap(dirn, j).wait_send()
            for s in range(stages):
                hop(dirn, s, j).wait_send()
            back(dirn, j).wait_send()
        each(half, body)

    def rows(b):
        return pl.ds(b * block, block)

    def key_sums(h):
        fetch(0, h).wait()
        fetch(1, h).wait()
        total = jnp.zeros((PAY, E), F32)
        for b in range(nblk):
            f = features(kv[h, rows(b), :])
            fk[h, rows(b), :] = f
            state = dot(f, vv[h, rows(b), :], 0, 0)
            norm = jnp.sum(f.astype(F32), axis=0, keepdims=True)
            part = jnp.concatenate([state, jnp.broadcast_to(norm, (8, E))], axis=0)
            kvb[h, b] = part
            total = total + part
        tot[0, h] = total

    def causal():
        return (lax.broadcasted_iota(jnp.int32, (tile, tile), 0)
                >= lax.broadcasted_iota(jnp.int32, (tile, tile), 1))

    def forward_local(h):
        fetch(2, h).wait()
        keep = causal()
        ones = jnp.ones((block, E), BF16)
        for b in range(nblk):
            base = b * block
            f = features(qv[h, rows(b), :])
            fq[h, rows(b), :] = f
            g = fk[h, rows(b), :]
            va = jnp.concatenate([vv[h, rows(b), :], ones], axis=1)
            top = jnp.where(keep, dot(f[:tile], g[:tile], 1, 1), 0.0).astype(BF16)
            low = dot(f[tile:], g, 1, 1)
            left = low[:, :tile].astype(BF16)
            right = jnp.where(keep, low[:, tile:], 0.0).astype(BF16)
            wts[h, b, 0] = top
            wts[h, b, 1] = left
            wts[h, b, 2] = right
            up = dot(top, va[:tile])
            down = dot(jnp.concatenate([left, right], axis=1), va)
            att[h, pl.ds(base, tile), :] = up[:, :E]
            den[h, pl.ds(base, tile), :] = up[:, E:]
            att[h, pl.ds(base + tile, tile), :] = down[:, :E]
            den[h, pl.ds(base + tile, tile), :] = down[:, E:]

    def forward_state(b):
        def body(h, sums):
            sq, pr = sums
            if b == 0:
                fetch(3, h).wait()
            full = pfx[0, h]
            for a in range(b):
                full = full + kvb[h, a]
            hi, lo = split(full[:E])
            sh[h, b] = jnp.concatenate([hi, lo], axis=1)
            norm = jnp.transpose(jnp.broadcast_to(full[NORM:NORM + 1], (E, E)))
            nhi, nlo = split(norm)
            wide = jnp.concatenate([jnp.concatenate([hi, nhi], axis=1),
                                    jnp.concatenate([lo, nlo], axis=1)], axis=0)
            f = fq[h, rows(b), :]
            both = dot(jnp.concatenate([f, f], axis=1), wide)
            inv = 1.0 / (den[h, rows(b), :] + both[:, E:])
            out = (att[h, rows(b), :] + both[:, :E]) * inv
            den[h, rows(b), :] = inv
            att[h, rows(b), :] = out
            w = cv[h, rows(b), :].astype(F32) * gain_ref[pl.ds(h, 1), :]
            return sq + out * out, pr + w * out
        zero = jnp.zeros((block, E), F32)
        sq, pr = lax.fori_loop(0, heads, body, (zero, zero))
        stat[b, 0:1, :] = jnp.sum(jnp.transpose(sq), axis=0, keepdims=True)
        stat[b, 1:2, :] = jnp.sum(jnp.transpose(pr), axis=0, keepdims=True)

    def share(b, d):
        return pltpu.make_async_remote_copy(
            src_ref=stat.at[b], dst_ref=stat_in.at[b, d - 1],
            send_sem=ss.at[b, d - 1], recv_sem=rs.at[b, d - 1],
            device_id=zpeer(d), device_id_type=MESH)

    def scales(b):
        for d in range(1, n_head):
            share(b, d).wait_recv()
        total = stat[b]
        for d in range(1, n_head):
            total = total + stat_in[b, d - 1]
        scale = lax.rsqrt(total[0:1] / width + 1e-06)
        pull = scale * scale * scale * total[1:2] / width
        scl[b, 0] = jnp.transpose(jnp.broadcast_to(scale, (E, block)))
        scl[b, 1] = jnp.transpose(jnp.broadcast_to(pull, (E, block)))

    def gradient(h):
        total = jnp.zeros((PAY, E), F32)
        gain = gain_ref[pl.ds(h, 1), :]
        for b in range(nblk):
            scale, pull = scl[b, 0], scl[b, 1]
            out, inv = att[h, rows(b), :], den[h, rows(b), :]
            sg = scale * gain
            om[h, rows(b), :] = (out * sg).astype(BF16)
            d = sg * cv[h, rows(b), :].astype(F32) - out * pull
            g = (d * inv).astype(BF16)
            gd = -jnp.sum(d * out, axis=1, keepdims=True) * inv
            gn[h, rows(b), :] = g
            den[h, rows(b), :] = gd
            f = fq[h, rows(b), :]
            later = dot(f, g, 0, 0)
            lden = jnp.sum(gd * f.astype(F32), axis=0, keepdims=True)
            part = jnp.concatenate([later, jnp.broadcast_to(lden, (8, E))], axis=0)
            rvb[h, b] = part
            total = total + part
        tot[1, h] = total
        put(0, h).start()

    def backward_local(h):
        keep = causal()
        for b in range(nblk):
            base = b * block
            f, k, v, g = fq[h, rows(b), :], fk[h, rows(b), :], vv[h, rows(b), :], gn[h, rows(b), :]
            gd = den[h, rows(b), :]
            gw = jnp.concatenate([gd] * (tile // E), axis=1)
            top = jnp.where(keep, dot(g[:tile], v[:tile], 1, 1) + gw[:tile], 0.0).astype(BF16)
            low = dot(g[tile:], v, 1, 1)
            left = (low[:, :tile] + gw[tile:]).astype(BF16)
            right = jnp.where(keep, low[:, tile:] + gw[tile:], 0.0).astype(BF16)
            norm = pfx[0, h, NORM:NORM + 1, :]
            for a in range(b):
                norm = norm + kvb[h, a, NORM:NORM + 1, :]
            far = dot(jnp.concatenate([g, g], axis=1), sh[h, b], 1, 1) + gd * norm
            up = dot(top, k[:tile]) + far[:tile]
            down = dot(jnp.concatenate([left, right], axis=1), k) + far[tile:]
            sl = slope(qv[h, rows(b), :])
            oq[h, pl.ds(base, tile), :] = (up * sl[:tile]).astype(BF16)
            oq[h, pl.ds(base + tile, tile), :] = (down * sl[tile:]).astype(BF16)
            att[h, pl.ds(base, tile), :] = dot(jnp.concatenate([top, left], axis=0), f, 0, 0)
            att[h, pl.ds(base + tile, tile), :] = dot(right, f[tile:], 0, 0)
            first = jnp.concatenate([wts[h, b, 0], wts[h, b, 1]], axis=0)
            dvp[h, pl.ds(base, tile), :] = dot(first, g, 0, 0)
            dvp[h, pl.ds(base + tile, tile), :] = dot(wts[h, b, 2], g[tile:], 0, 0)
        put(1, h).start()

    def backward_state(h):
        for b in range(nblk):
            full = pfx[1, h]
            for a in range(b + 1, nblk):
                full = full + rvb[h, a]
            hi, lo = split(full[:E])
            v, k = vv[h, rows(b), :], fk[h, rows(b), :]
            dk = dot(jnp.concatenate([v, v], axis=1), jnp.concatenate([hi, lo], axis=1), 1, 1)
            dk = dk + att[h, rows(b), :] + full[NORM:NORM + 1]
            ok[h, rows(b), :] = (dk * slope(kv[h, rows(b), :])).astype(BF16)
            dv = dot(jnp.concatenate([k, k], axis=1), jnp.concatenate([hi, lo], axis=0))
            ov[h, rows(b), :] = (dv + dvp[h, rows(b), :]).astype(BF16)
        put(2, h).start()
        put(3, h).start()

    def middle(dirn, local):
        chip_total(dirn)
        per = heads // (stages + 1)
        at = 0
        for s in range(stages):
            low, count = at, per
            at += per
            each(count, lambda j, low=low: local(low + j))
            hop_on(dirn, s)
        each(heads - at, lambda j: local(at + j))
        arrive(dirn)

    def theirs_first(dirn, body):
        def one(j):
            body(theirs + j)
            swap(dirn, j).start()
        each(half, one)
        each(half, lambda j: body(mine + j))

    greeted = len(masks) + n_head - 1

    def one_ready(j):
        key_sums(theirs + j)

    each(half, one_ready)
    pl.semaphore_wait(barrier, greeted)
    each(half, lambda j: swap(0, j).start())
    each(half, lambda j: key_sums(mine + j))
    middle(0, forward_local)
    for b in range(nblk):
        forward_state(b)
        for d in range(1, n_head):
            share(b, d).start()
    for b in range(nblk):
        scales(b)
    theirs_first(1, gradient)
    middle(1, backward_local)
    each(heads, backward_state)

    drain(0)
    drain(1)
    for b in range(nblk):
        for d in range(1, n_head):
            share(b, d).wait_send()

    def finish(h):
        for array in range(4):
            put(array, h).wait()
    each(heads, finish)


def shards(sizes, queries, keys, values, gain, cotangent):
    n_in, n_out, n_head = sizes
    rows, width = queries.shape
    heads = width // E
    block = min(BLOCK, rows)
    nblk = rows // block
    half = heads // 2
    stages = max((n_in * n_out // 2).bit_length() - 1, 1)
    dims = (heads, nblk, block, n_in, n_out, n_head, width * n_head)
    whole = (heads, rows, E)
    anywhere = pl.BlockSpec(memory_space=pl.ANY)
    dma = pltpu.SemaphoreType.DMA
    scratch = [pltpu.VMEM(whole, BF16) for _ in range(4)]
    scratch += [pltpu.VMEM(whole, BF16) for _ in range(2)]
    scratch += [
        pltpu.VMEM((heads, nblk, 3, block // 2, block // 2), BF16),
        pltpu.VMEM(whole, F32),
        pltpu.VMEM(whole, F32),
        pltpu.VMEM(whole, BF16),
        pltpu.VMEM(whole, F32),
    ]
    scratch += [pltpu.VMEM(whole, BF16) for _ in range(4)]
    scratch += [
        pltpu.VMEM((heads, nblk, PAY, E), F32),
        pltpu.VMEM((heads, nblk, PAY, E), F32),
        pltpu.VMEM((heads, nblk, E, 2 * E), BF16),
        pltpu.VMEM((2, heads, PAY, E), F32),
        pltpu.VMEM((2, half, PAY, E), F32),
        pltpu.VMEM((2, stages, half, PAY, E), F32),
        pltpu.VMEM((2, stages, half, PAY, E), F32),
        pltpu.VMEM((2, half, PAY, E), F32),
        pltpu.VMEM((2, heads, PAY, E), F32),
        pltpu.VMEM((nblk, 2, block), F32),
        pltpu.VMEM((nblk, n_head - 1, 2, block), F32),
        pltpu.VMEM((nblk, 2, block, E), F32),
        dma((4, heads)),
        dma((4, heads)),
        dma((2, half)),
        dma((2, half)),
        dma((2, stages, half)),
        dma((2, stages, half)),
        dma((2, half)),
        dma((2, half)),
        dma((nblk, n_head - 1)),
        dma((nblk, n_head - 1)),
    ]
    out = jax.ShapeDtypeStruct((rows, width), BF16)
    return pl.pallas_call(
        functools.partial(kernel, dims),
        out_shape=(out,) * 4,
        in_specs=[anywhere, anywhere, anywhere, pl.BlockSpec(memory_space=pltpu.VMEM), anywhere],
        out_specs=(anywhere,) * 4,
        scratch_shapes=scratch,
        compiler_params=pltpu.CompilerParams(
            collective_id=0, has_side_effects=True, vmem_limit_bytes=60 * 1024 * 1024
        ),
        cost_estimate=pl.CostEstimate(
            flops=16 * rows * block * width, bytes_accessed=16 * rows * width,
            transcendentals=4 * rows * width,
        ),
    )(queries, keys, values, gain.reshape(heads, E), cotangent)


def solution(mesh):
    sizes = tuple(mesh.shape[name] for name in ("seqin", "seqout", "head"))
    rows = P(("seqin", "seqout"), "head")
    return jax.shard_map(
        functools.partial(shards, sizes),
        mesh=mesh,
        in_specs=(rows, rows, rows, P("head"), rows),
        out_specs=(rows,) * 4,
        check_vma=False,
    )
```

profile of v0, /device:TPU:0, one launch (start us, length us, event | category | flops | bytes accessed | tf_op | source)
XLA Modules:
  0.0 65.9 jit_solution(5803316020448445409)
XLA Ops:
  0.6 56.0 %shard_map.84 = (bf16[1024,1024]{1,0:T(8,128)(2,1)}, bf16[1024,1024]{1,0:T(8,128)(2,1)}, bf16[1024,1024]{1,0:T(8,128)(2,1)}, bf16[1024,1024]{1,0:T(8,128)(2,1)}) custom-call(bf16[1024,1024]{1,0:T(8,128)(2,1)} %q_hbm.1, bf16[1024,1024]{1,0:T(8,128)(2,1)} %k_hbm.1, bf16[1024,1024]{1,0:T(8,128)(2,1)} %v_hbm.1, f32[8,128]{1,0:T(8,128)} %bitcast.1, ...), custom_call_target="tpu_custom_call" | custom-call | flops 8589934592 | bytes 16777216 | tf_op jit(solution)/shard_map/pallas_call | solution.py:411
  56.6 0.0 copy-start.2
  56.6 3.2 %copy.13 = bf16[1024,1024]{1,0:T(8,128)(2,1)} copy(bf16[1024,1024]{1,0:T(8,128)(2,1)} %get-tuple-element.8) | data formatting | bytes 4194304
  59.8 0.0 copy-done.2
  59.8 0.0 copy-start.1
  59.8 1.3 %copy.14 = bf16[1024,1024]{1,0:T(8,128)(2,1)} copy(bf16[1024,1024]{1,0:T(8,128)(2,1)S(1)} %copy-done.2) | data formatting | bytes 4194304
  61.2 1.0 %copy-done.1 = bf16[1024,1024]{1,0:T(8,128)(2,1)S(1)} copy-done((bf16[1024,1024]{1,0:T(8,128)(2,1)S(1)}, bf16[1024,1024]{1,0:T(8,128)(2,1)}, u32[]{:S(2)}) %copy-start.1) | copy-done | bytes 2097176
  62.2 0.0 copy-start
  62.2 1.3 %copy.15 = bf16[1024,1024]{1,0:T(8,128)(2,1)} copy(bf16[1024,1024]{1,0:T(8,128)(2,1)S(1)} %copy-done.1) | data formatting | bytes 4194304
  63.5 1.0 %copy-done = bf16[1024,1024]{1,0:T(8,128)(2,1)S(1)} copy-done((bf16[1024,1024]{1,0:T(8,128)(2,1)S(1)}, bf16[1024,1024]{1,0:T(8,128)(2,1)}, u32[]{:S(2)}) %copy-start) | copy-done | bytes 2097176
  64.5 1.3 %copy.16 = bf16[1024,1024]{1,0:T(8,128)(2,1)} copy(bf16[1024,1024]{1,0:T(8,128)(2,1)S(1)} %copy-done) | data formatting | bytes 4194304
Async XLA Ops:
  56.6 3.2 %copy-start.2 = (bf16[1024,1024]{1,0:T(8,128)(2,1)S(1)}, bf16[1024,1024]{1,0:T(8,128)(2,1)}, u32[]{:S(2)}) copy-start(bf16[1024,1024]{1,0:T(8,128)(2,1)} %get-tuple-element.9) | copy-start | bytes 6291460
  59.8 2.3 %copy-start.1 = (bf16[1024,1024]{1,0:T(8,128)(2,1)S(1)}, bf16[1024,1024]{1,0:T(8,128)(2,1)}, u32[]{:S(2)}) copy-start(bf16[1024,1024]{1,0:T(8,128)(2,1)} %get-tuple-element.10) | copy-start | bytes 6291460
  62.2 2.3 %copy-start = (bf16[1024,1024]{1,0:T(8,128)(2,1)S(1)}, bf16[1024,1024]{1,0:T(8,128)(2,1)}, u32[]{:S(2)}) copy-start(bf16[1024,1024]{1,0:T(8,128)(2,1)} %get-tuple-element.11) | copy-start | bytes 6291460
where the time goes:
time: 66.1 us; the launch traced here: 65.9 us
  Pallas kernels  56 us (85%)
  local copies, waits for them, and re-layouts  9.25 us (14%)
    pallas_call x1, Pallas kernels, shards(): pl.pallas_call(functools.partial(kernel, dims), out_shape=(out,) * 4, in_...  56 us
    unnamed x10, local copies, waits for them, and re-layouts  9.25 us

commit v1 on v0

--- a/solution.py
+++ b/solution.py
@@ -13,6 +13,8 @@
 PAY = E + 8
 F32 = jnp.float32
 BF16 = jnp.bfloat16
+VMEM_A = 34 * 1024 * 1024
+VMEM_B = 8 * 1024 * 1024
 MESH = pl.DeviceIdType.MESH
 
 
@@ -34,10 +36,16 @@
     return hi, (x - hi.astype(F32)).astype(BF16)
 
 
-def kernel(dims, q_hbm, k_hbm, v_hbm, gain_ref, c_hbm, mixed_hbm, gq_hbm, gk_hbm, gv_hbm,
-           qv, kv, vv, cv, fq, fk, wts, att, den, gn, dvp, om, oq, ok, ov,
-           kvb, rvb, sh, tot, r0, tx, rx, fin, pfx, stat, stat_in, scl,
-           in_sem, out_sem, s0, q0, sx, rxs, s2, q2, ss, rs):
+def each(n, body):
+    def step(j, carry):
+        body(j)
+        return carry
+    lax.fori_loop(0, n, step, 0)
+
+
+def kernel(dims, q_hbm, k_hbm, v_hbm, gain_ref, c_hbm, om, oq, kv, vv, fk, att, dvp, lat,
+           qv, cv, fq, wts, den, gn, kvb, rvb, sh, tot, r0, tx, rx, fin, pfx, stat, stat_in, scl,
+           in_sem, s0, q0, sx, rxs, s2, q2, ss, rs):
     heads, nblk, block, n_in, n_out, n_head, width = dims
     half = heads // 2
     tile = block // 2
@@ -64,17 +72,6 @@
         src, dst = ((k_hbm, kv), (v_hbm, vv), (q_hbm, qv), (c_hbm, cv))[array]
         cols = pl.ds(pl.multiple_of(h * E, E), E)
         return pltpu.make_async_copy(src.at[:, cols], dst.at[h], in_sem.at[array, h])
-
-    def put(array, h):
-        src, dst = ((om, mixed_hbm), (oq, gq_hbm), (ok, gk_hbm), (ov, gv_hbm))[array]
-        cols = pl.ds(pl.multiple_of(h * E, E), E)
-        return pltpu.make_async_copy(src.at[h], dst.at[:, cols], out_sem.at[array, h])
-
-    def each(n, body):
-        def step(j, carry):
-            body(j)
-            return carry
-        lax.fori_loop(0, n, step, 0)
 
     def order(j):
         return lax.rem(theirs + j, heads)
@@ -266,7 +263,6 @@
             rvb[h, b] = part
             total = total + part
         tot[1, h] = total
-        put(0, h).start()
 
     def backward_local(h):
         keep = causal()
@@ -293,22 +289,12 @@
             first = jnp.concatenate([wts[h, b, 0], wts[h, b, 1]], axis=0)
             dvp[h, pl.ds(base, tile), :] = dot(first, g, 0, 0)
             dvp[h, pl.ds(base + tile, tile), :] = dot(wts[h, b, 2], g[tile:], 0, 0)
-        put(1, h).start()
-
-    def backward_state(h):
-        for b in range(nblk):
-            full = pfx[1, h]
-            for a in range(b + 1, nblk):
-                full = full + rvb[h, a]
-            hi, lo = split(full[:E])
-            v, k = vv[h, rows(b), :], fk[h, rows(b), :]
-            dk = dot(jnp.concatenate([v, v], axis=1), jnp.concatenate([hi, lo], axis=1), 1, 1)
-            dk = dk + att[h, rows(b), :] + full[NORM:NORM + 1]
-            ok[h, rows(b), :] = (dk * slope(kv[h, rows(b), :])).astype(BF16)
-            dv = dot(jnp.concatenate([k, k], axis=1), jnp.concatenate([hi, lo], axis=0))
-            ov[h, rows(b), :] = (dv + dvp[h, rows(b), :]).astype(BF16)
-        put(2, h).start()
-        put(3, h).start()
+
+    def later_sums(h):
+        full = pfx[1, h]
+        for b in reversed(range(nblk)):
+            lat[h, b] = full
+            full = full + rvb[h, b]
 
     def middle(dirn, local):
         chip_total(dirn)
@@ -347,7 +333,7 @@
         scales(b)
     theirs_first(1, gradient)
     middle(1, backward_local)
-    each(heads, backward_state)
+    each(heads, later_sums)
 
     drain(0)
     drain(1)
@@ -355,9 +341,40 @@
         for d in range(1, n_head):
             share(b, d).wait_send()
 
+
+def last(dims, om, oq, kv, vv, fk, att, dvp, lat, mixed_hbm, gq_hbm, gk_hbm, gv_hbm,
+         ok, ov, out_sem):
+    heads, nblk, block = dims[:3]
+
+    def put(array, h):
+        src, dst = ((om, mixed_hbm), (oq, gq_hbm), (ok, gk_hbm), (ov, gv_hbm))[array]
+        cols = pl.ds(pl.multiple_of(h * E, E), E)
+        return pltpu.make_async_copy(src.at[h], dst.at[:, cols], out_sem.at[array, h])
+
+    def ready(h):
+        put(0, h).start()
+        put(1, h).start()
+
+    def backward_state(h):
+        for b in range(nblk):
+            rows = pl.ds(b * block, block)
+            full = lat[h, b]
+            hi, lo = split(full[:E])
+            v, k = vv[h, rows, :], fk[h, rows, :]
+            dk = dot(jnp.concatenate([v, v], axis=1), jnp.concatenate([hi, lo], axis=1), 1, 1)
+            dk = dk + att[h, rows, :] + full[NORM:NORM + 1]
+            ok[h, rows, :] = (dk * slope(kv[h, rows, :])).astype(BF16)
+            dv = dot(jnp.concatenate([k, k], axis=1), jnp.concatenate([hi, lo], axis=0))
+            ov[h, rows, :] = (dv + dvp[h, rows, :]).astype(BF16)
+        put(2, h).start()
+        put(3, h).start()
+
     def finish(h):
         for array in range(4):
             put(array, h).wait()
+
+    each(heads, ready)
+    each(heads, backward_state)
     each(heads, finish)
 
 
@@ -373,17 +390,15 @@
     whole = (heads, rows, E)
     anywhere = pl.BlockSpec(memory_space=pl.ANY)
     dma = pltpu.SemaphoreType.DMA
-    scratch = [pltpu.VMEM(whole, BF16) for _ in range(4)]
-    scratch += [pltpu.VMEM(whole, BF16) for _ in range(2)]
-    scratch += [
+    half16, full32 = pltpu.VMEM(whole, BF16), pltpu.VMEM(whole, F32)
+    held = (half16,) * 5 + (full32,) * 2 + (pltpu.VMEM((heads, nblk, PAY, E), F32),)
+    scratch = [
+        half16,
+        half16,
+        half16,
         pltpu.VMEM((heads, nblk, 3, block // 2, block // 2), BF16),
-        pltpu.VMEM(whole, F32),
-        pltpu.VMEM(whole, F32),
-        pltpu.VMEM(whole, BF16),
-        pltpu.VMEM(whole, F32),
-    ]
-    scratch += [pltpu.VMEM(whole, BF16) for _ in range(4)]
-    scratch += [
+        full32,
+        half16,
         pltpu.VMEM((heads, nblk, PAY, E), F32),
         pltpu.VMEM((heads, nblk, PAY, E), F32),
         pltpu.VMEM((heads, nblk, E, 2 * E), BF16),
@@ -397,7 +412,6 @@
         pltpu.VMEM((nblk, n_head - 1, 2, block), F32),
         pltpu.VMEM((nblk, 2, block, E), F32),
         dma((4, heads)),
-        dma((4, heads)),
         dma((2, half)),
         dma((2, half)),
         dma((2, stages, half)),
@@ -407,21 +421,34 @@
         dma((nblk, n_head - 1)),
         dma((nblk, n_head - 1)),
     ]
-    out = jax.ShapeDtypeStruct((rows, width), BF16)
-    return pl.pallas_call(
+    inside = pl.BlockSpec(memory_space=pltpu.VMEM)
+    kept = pl.pallas_call(
         functools.partial(kernel, dims),
-        out_shape=(out,) * 4,
-        in_specs=[anywhere, anywhere, anywhere, pl.BlockSpec(memory_space=pltpu.VMEM), anywhere],
-        out_specs=(anywhere,) * 4,
+        out_shape=held,
+        in_specs=[anywhere, anywhere, anywhere, inside, anywhere],
+        out_specs=(inside,) * len(held),
         scratch_shapes=scratch,
         compiler_params=pltpu.CompilerParams(
-            collective_id=0, has_side_effects=True, vmem_limit_bytes=60 * 1024 * 1024
+            collective_id=0, has_side_effects=True, vmem_limit_bytes=VMEM_A
         ),
         cost_estimate=pl.CostEstimate(
-            flops=16 * rows * block * width, bytes_accessed=16 * rows * width,
+            flops=16 * rows * block * width, bytes_accessed=8 * rows * width,
             transcendentals=4 * rows * width,
         ),
     )(queries, keys, values, gain.reshape(heads, E), cotangent)
+    out = jax.ShapeDtypeStruct((rows, width), BF16)
+    return pl.pallas_call(
+        functools.partial(last, dims),
+        out_shape=(out,) * 4,
+        in_specs=[inside] * len(held),
+        out_specs=(anywhere,) * 4,
+        scratch_shapes=[half16, half16, dma((4, heads))],
+        compiler_params=pltpu.CompilerParams(vmem_limit_bytes=VMEM_B),
+        cost_estimate=pl.CostEstimate(
+            flops=4 * rows * 2 * E * width, bytes_accessed=8 * rows * width,
+            transcendentals=rows * width,
+        ),
+    )(*kept)
 
 
 def solution(mesh):

time: 66.1 us -> 57.3 us (0.87)
  local copies, waits for them, and re-layouts: 9.25 us -> 0.68 us
    unnamed x10 -> x2, local copies, waits for them, and re-layouts: 9.25 us -> 0.68 us
    pallas_call x1 -> x2, Pallas kernels: 56 us -> 55.8 us  [the longest x1 51.1 us: shards(): pl.pallas_call(functools.partial(kernel, dims), out_shape=held, in_specs=...]
where the time goes in v1:
time: 57.3 us; the launch traced here: 57.1 us
  Pallas kernels  55.8 us (97%)
  local copies, waits for them, and re-layouts  0.68 us (1%)
  between operations  0.65 us (1%)
    pallas_call x1, Pallas kernels, shards(): pl.pallas_call(functools.partial(kernel, dims), out_shape=held, in_specs=...  51.1 us
    pallas_call x1, Pallas kernels, shards(): pl.pallas_call(functools.partial(last, dims), out_shape=(out,) * 4, in_sp...  4.72 us

profile of v1, /device:TPU:0, one launch (start us, length us, event | category | flops | bytes accessed | tf_op | source)
XLA Modules:
  0.0 57.1 jit_solution(4173056891549417186)
XLA Ops:
  0.6 0.0 copy-start
  0.6 0.7 %copy-done = f32[1024]{0:T(1024)S(1)} copy-done((f32[1024]{0:T(1024)S(1)}, f32[1024]{0:T(1024)}, u32[]{:S(2)}) %copy-start) | copy-done | bytes 4120
  1.3 51.1 %shard_map.84 = (bf16[8,1024,128]{2,1,0:T(8,128)(2,1)S(1)}, bf16[8,1024,128]{2,1,0:T(8,128)(2,1)S(1)}, bf16[8,1024,128]{2,1,0:T(8,128)(2,1)S(1)}, bf16[8,1024,12...) custom-call(bf16[1024,1024]{1,0:T(8,128)(2,1)} %q_hbm.1, ...), custom_call_target="tpu_custom_call" | custom-call | flops 8589934592 | bytes 8388608 | tf_op jit(solution)/shard_map/pallas_call | solution.py:425
  52.4 4.7 %shard_map.85 = (bf16[1024,1024]{1,0:T(8,128)(2,1)}, bf16[1024,1024]{1,0:T(8,128)(2,1)}, bf16[1024,1024]{1,0:T(8,128)(2,1)}, bf16[1024,1024]{1,0:T(8,128)(2,1)}) custom-call(bf16[8,1024,128]{2,1,0:T(8,128)(2,1)S(1)} %get-tuple-element.12.om, bf16[8,1024,128]{2,1,0:T(8,128)(2,1)S(1)} %get-tuple-element.13.oq, bf16[8,1024,128]{2,1,0:T(8,128)(2,1)S(1)} %get-tuple-element.14.kv, ...), custom_call_target="tpu_custom_call" | custom-call | flops 1073741824 | bytes 8388608 | tf_op jit(solution)/shard_map/pallas_call | solution.py:440
Async XLA Ops:
  0.6 0.7 %copy-start = (f32[1024]{0:T(1024)S(1)}, f32[1024]{0:T(1024)}, u32[]{:S(2)}) copy-start(f32[1024]{0:T(1024)} %param.8) | copy-start | bytes 12292

commit v2 on v1

--- a/solution.py
+++ b/solution.py
@@ -43,9 +43,9 @@
     lax.fori_loop(0, n, step, 0)
 
 
-def kernel(dims, q_hbm, k_hbm, v_hbm, gain_ref, c_hbm, om, oq, kv, vv, fk, att, dvp, lat,
+def kernel(dims, q_hbm, k_hbm, v_hbm, g_hbm, c_hbm, om, oq, kv, vv, fk, att, dvp, lat,
            qv, cv, fq, wts, den, gn, kvb, rvb, sh, tot, r0, tx, rx, fin, pfx, stat, stat_in, scl,
-           in_sem, s0, q0, sx, rxs, s2, q2, ss, rs):
+           gain_ref, gain_sem, in_sem, s0, q0, sx, rxs, s2, q2, ss, rs):
     heads, nblk, block, n_in, n_out, n_head, width = dims
     half = heads // 2
     tile = block // 2
@@ -73,19 +73,19 @@
         cols = pl.ds(pl.multiple_of(h * E, E), E)
         return pltpu.make_async_copy(src.at[:, cols], dst.at[h], in_sem.at[array, h])
 
-    def order(j):
-        return lax.rem(theirs + j, heads)
-
     def start_kv(j):
-        fetch(0, order(j)).start()
-        fetch(1, order(j)).start()
+        for h in (theirs + j, mine + j):
+            fetch(0, h).start()
+            fetch(1, h).start()
 
     def start_qc(h):
         fetch(2, h).start()
-        fetch(3, h).start()
-
-    each(heads, start_kv)
+
+    each(half, start_kv)
     each(heads, start_qc)
+    each(heads, lambda h: fetch(3, h).start())
+    gain_copy = pltpu.make_async_copy(g_hbm, gain_ref, gain_sem)
+    gain_copy.start()
 
     barrier = pltpu.get_barrier_semaphore()
     masks = [1 << s for s in range(stages + 1)]
@@ -118,30 +118,26 @@
             send_sem=s2.at[dirn, j], recv_sem=q2.at[dirn, j],
             device_id=peer(1), device_id_type=MESH)
 
-    def chip_total(dirn):
-        def body(j):
-            swap(dirn, j).wait_recv()
-            tx[dirn, 0, j] = tot[dirn, mine + j] + r0[dirn, j]
-            hop(dirn, 0, j).start()
-        each(half, body)
-
-    def hop_on(dirn, s):
-        def body(j):
-            hop(dirn, s, j).wait_recv()
-            if s + 1 < stages:
-                tx[dirn, s + 1, j] = tx[dirn, s, j] + rx[dirn, s, j]
-                hop(dirn, s + 1, j).start()
-                return
-            total = jnp.zeros((PAY, E), F32)
-            for i in range(stages):
-                before = bit(2 << i) == 1 - dirn
-                total = total + jnp.where(before, rx[dirn, i, j], 0.0)
-            near = core == dirn
-            own, other = tot[dirn, mine + j], r0[dirn, j]
-            fin[dirn, j] = total + jnp.where(near, own, 0.0)
-            pfx[dirn, mine + j] = total + jnp.where(near, 0.0, other)
-            back(dirn, j).start()
-        each(half, body)
+    def chip_total(dirn, j):
+        swap(dirn, j).wait_recv()
+        tx[dirn, 0, j] = tot[dirn, mine + j] + r0[dirn, j]
+        hop(dirn, 0, j).start()
+
+    def hop_on(dirn, s, j):
+        hop(dirn, s, j).wait_recv()
+        if s + 1 < stages:
+            tx[dirn, s + 1, j] = tx[dirn, s, j] + rx[dirn, s, j]
+            hop(dirn, s + 1, j).start()
+            return
+        total = jnp.zeros((PAY, E), F32)
+        for i in range(stages):
+            before = bit(2 << i) == 1 - dirn
+            total = total + jnp.where(before, rx[dirn, i, j], 0.0)
+        near = core == dirn
+        own, other = tot[dirn, mine + j], r0[dirn, j]
+        fin[dirn, j] = total + jnp.where(near, own, 0.0)
+        pfx[dirn, mine + j] = total + jnp.where(near, 0.0, other)
+        back(dirn, j).start()
 
     def arrive(dirn):
         each(half, lambda j: back_in(dirn, j).wait_recv())
@@ -243,26 +239,23 @@
         scl[b, 0] = jnp.transpose(jnp.broadcast_to(scale, (E, block)))
         scl[b, 1] = jnp.transpose(jnp.broadcast_to(pull, (E, block)))
 
-    def gradient(h):
-        total = jnp.zeros((PAY, E), F32)
+    def gradient(b, h):
         gain = gain_ref[pl.ds(h, 1), :]
-        for b in range(nblk):
-            scale, pull = scl[b, 0], scl[b, 1]
-            out, inv = att[h, rows(b), :], den[h, rows(b), :]
-            sg = scale * gain
-            om[h, rows(b), :] = (out * sg).astype(BF16)
-            d = sg * cv[h, rows(b), :].astype(F32) - out * pull
-            g = (d * inv).astype(BF16)
-            gd = -jnp.sum(d * out, axis=1, keepdims=True) * inv
-            gn[h, rows(b), :] = g
-            den[h, rows(b), :] = gd
-            f = fq[h, rows(b), :]
-            later = dot(f, g, 0, 0)
-            lden = jnp.sum(gd * f.astype(F32), axis=0, keepdims=True)
-            part = jnp.concatenate([later, jnp.broadcast_to(lden, (8, E))], axis=0)
-            rvb[h, b] = part
-            total = total + part
-        tot[1, h] = total
+        scale, pull = scl[b, 0], scl[b, 1]
+        out, inv = att[h, rows(b), :], den[h, rows(b), :]
+        sg = scale * gain
+        om[h, rows(b), :] = (out * sg).astype(BF16)
+        d = sg * cv[h, rows(b), :].astype(F32) - out * pull
+        g = (d * inv).astype(BF16)
+        gd = -jnp.sum(d * out, axis=1, keepdims=True) * inv
+        gn[h, rows(b), :] = g
+        den[h, rows(b), :] = gd
+        f = fq[h, rows(b), :]
+        later = dot(f, g, 0, 0)
+        lden = jnp.sum(gd * f.astype(F32), axis=0, keepdims=True)
+        part = jnp.concatenate([later, jnp.broadcast_to(lden, (8, E))], axis=0)
+        rvb[h, b] = part
+        tot[1, h] = tot[1, h] + part if b else part
 
     def backward_local(h):
         keep = causal()
@@ -296,43 +289,52 @@
             lat[h, b] = full
             full = full + rvb[h, b]
 
-    def middle(dirn, local):
-        chip_total(dirn)
-        per = heads // (stages + 1)
-        at = 0
-        for s in range(stages):
-            low, count = at, per
-            at += per
-            each(count, lambda j, low=low: local(low + j))
-            hop_on(dirn, s)
-        each(heads - at, lambda j: local(at + j))
+    def sums(dirn, body, greet=None):
+        body(theirs)
+        if greet is not None:
+            greet()
+        swap(dirn, 0).start()
+
+        def step(j):
+            body(mine + j)
+
+            @pl.when(j < half - 1)
+            def _():
+                body(theirs + j + 1)
+                swap(dirn, j + 1).start()
+            chip_total(dirn, j)
+        each(half, step)
+
+    def middle(dirn, local, slot):
+        events = sorted((slot(s, j), s, j) for s in range(stages) for j in range(half))
+
+        def step(h):
+            local(h)
+            for at, s, j in events:
+                if at < heads:
+                    @pl.when(h == at)
+                    def _(s=s, j=j):
+                        hop_on(dirn, s, j)
+        each(heads, step)
+        for at, s, j in events:
+            if at >= heads:
+                hop_on(dirn, s, j)
         arrive(dirn)
 
-    def theirs_first(dirn, body):
-        def one(j):
-            body(theirs + j)
-            swap(dirn, j).start()
-        each(half, one)
-        each(half, lambda j: body(mine + j))
-
     greeted = len(masks) + n_head - 1
-
-    def one_ready(j):
-        key_sums(theirs + j)
-
-    each(half, one_ready)
-    pl.semaphore_wait(barrier, greeted)
-    each(half, lambda j: swap(0, j).start())
-    each(half, lambda j: key_sums(mine + j))
-    middle(0, forward_local)
+    sums(0, key_sums, lambda: pl.semaphore_wait(barrier, greeted))
+    middle(0, forward_local, lambda s, j: 1 + (3 * j) // 2 + 4 * s)
+    gain_copy.wait()
     for b in range(nblk):
         forward_state(b)
         for d in range(1, n_head):
             share(b, d).start()
-    for b in range(nblk):
+    for b in range(nblk - 1):
         scales(b)
-    theirs_first(1, gradient)
-    middle(1, backward_local)
+        each(heads, functools.partial(gradient, b))
+    scales(nblk - 1)
+    sums(1, functools.partial(gradient, nblk - 1))
+    middle(1, backward_local, lambda s, j: j + 2 * s)
     each(heads, later_sums)
 
     drain(0)
@@ -411,6 +413,8 @@
         pltpu.VMEM((nblk, 2, block), F32),
         pltpu.VMEM((nblk, n_head - 1, 2, block), F32),
         pltpu.VMEM((nblk, 2, block, E), F32),
+        pltpu.VMEM((heads, E), F32),
+        dma,
         dma((4, heads)),
         dma((2, half)),
         dma((2, half)),
@@ -425,7 +429,7 @@
     kept = pl.pallas_call(
         functools.partial(kernel, dims),
         out_shape=held,
-        in_specs=[anywhere, anywhere, anywhere, inside, anywhere],
+        in_specs=[pl.BlockSpec(memory_space=pltpu.MemorySpace.HBM)] * 5,
         out_specs=(inside,) * len(held),
         scratch_shapes=scratch,
         compiler_params=pltpu.CompilerParams(

time: 57.3 us -> 53 us (0.925)
  Pallas kernels: 55.8 us -> 51.5 us
    pallas_call x1, Pallas kernels: 51.1 us -> 46.8 us  [shards(): pl.pallas_call(functools.partial(kernel, dims), out_shape=held, in_specs=...]
where the time goes in v2:
time: 53 us; the launch traced here: 52.8 us
  Pallas kernels  51.5 us (97%)
  local copies, waits for them, and re-layouts  0.68 us (1%)
  between operations  0.65 us (1%)
    pallas_call x1, Pallas kernels, shards(): pl.pallas_call(functools.partial(kernel, dims), out_shape=held, in_specs=...  46.8 us
    pallas_call x1, Pallas kernels, shards(): pl.pallas_call(functools.partial(last, dims), out_shape=(out,) * 4, in_sp...  4.73 us

profile of v2, /device:TPU:0, one launch (start us, length us, event | category | flops | bytes accessed | tf_op | source)
XLA Modules:
  0.0 52.8 jit_solution(15296164673289437586)
XLA Ops:
  0.6 0.0 copy-start
  0.6 0.7 %copy-done = f32[1024]{0:T(1024)S(1)} copy-done((f32[1024]{0:T(1024)S(1)}, f32[1024]{0:T(1024)}, u32[]{:S(2)}) %copy-start) | copy-done | bytes 4120
  1.3 46.8 %shard_map.84 = (bf16[8,1024,128]{2,1,0:T(8,128)(2,1)S(1)}, bf16[8,1024,128]{2,1,0:T(8,128)(2,1)S(1)}, bf16[8,1024,128]{2,1,0:T(8,128)(2,1)S(1)}, bf16[8,1024,12...) custom-call(bf16[1024,1024]{1,0:T(8,128)(2,1)} %q_hbm.1, ...), custom_call_target="tpu_custom_call" | custom-call | flops 8589934592 | bytes 8388608 | tf_op jit(solution)/shard_map/pallas_call | solution.py:429
  48.1 4.7 %shard_map.85 = (bf16[1024,1024]{1,0:T(8,128)(2,1)}, bf16[1024,1024]{1,0:T(8,128)(2,1)}, bf16[1024,1024]{1,0:T(8,128)(2,1)}, bf16[1024,1024]{1,0:T(8,128)(2,1)}) custom-call(bf16[8,1024,128]{2,1,0:T(8,128)(2,1)S(1)} %get-tuple-element.12.om, bf16[8,1024,128]{2,1,0:T(8,128)(2,1)S(1)} %get-tuple-element.13.oq, bf16[8,1024,128]{2,1,0:T(8,128)(2,1)S(1)} %get-tuple-element.14.kv, ...), custom_call_target="tpu_custom_call" | custom-call | flops 1073741824 | bytes 8388608 | tf_op jit(solution)/shard_map/pallas_call | solution.py:444
Async XLA Ops:
  0.6 0.7 %copy-start = (f32[1024]{0:T(1024)S(1)}, f32[1024]{0:T(1024)}, u32[]{:S(2)}) copy-start(f32[1024]{0:T(1024)} %param.8) | copy-start | bytes 12292

commit v3 on v2

--- a/solution.py
+++ b/solution.py
@@ -8,7 +8,7 @@
 from jax.sharding import PartitionSpec as P
 
 E = 128
-BLOCK = 512
+BLOCK = 256
 NORM = E
 PAY = E + 8
 F32 = jnp.float32
@@ -44,11 +44,10 @@
 
 
 def kernel(dims, q_hbm, k_hbm, v_hbm, g_hbm, c_hbm, om, oq, kv, vv, fk, att, dvp, lat,
-           qv, cv, fq, wts, den, gn, kvb, rvb, sh, tot, r0, tx, rx, fin, pfx, stat, stat_in, scl,
+           qv, cv, fq, wts, den, gn, kvb, rvb, sh, tot, r0, tx, rx, fin, pfx, stat, stat_in, acc, nrm,
            gain_ref, gain_sem, in_sem, s0, q0, sx, rxs, s2, q2, ss, rs):
     heads, nblk, block, n_in, n_out, n_head, width = dims
     half = heads // 2
-    tile = block // 2
     n_seq = n_in * n_out
     nchips = n_seq // 2
     stages = nchips.bit_length() - 1
@@ -168,120 +167,109 @@
         tot[0, h] = total
 
     def causal():
-        return (lax.broadcasted_iota(jnp.int32, (tile, tile), 0)
-                >= lax.broadcasted_iota(jnp.int32, (tile, tile), 1))
+        return (lax.broadcasted_iota(jnp.int32, (block, block), 0)
+                >= lax.broadcasted_iota(jnp.int32, (block, block), 1))
 
     def forward_local(h):
         fetch(2, h).wait()
         keep = causal()
         ones = jnp.ones((block, E), BF16)
         for b in range(nblk):
-            base = b * block
             f = features(qv[h, rows(b), :])
             fq[h, rows(b), :] = f
-            g = fk[h, rows(b), :]
-            va = jnp.concatenate([vv[h, rows(b), :], ones], axis=1)
-            top = jnp.where(keep, dot(f[:tile], g[:tile], 1, 1), 0.0).astype(BF16)
-            low = dot(f[tile:], g, 1, 1)
-            left = low[:, :tile].astype(BF16)
-            right = jnp.where(keep, low[:, tile:], 0.0).astype(BF16)
-            wts[h, b, 0] = top
-            wts[h, b, 1] = left
-            wts[h, b, 2] = right
-            up = dot(top, va[:tile])
-            down = dot(jnp.concatenate([left, right], axis=1), va)
-            att[h, pl.ds(base, tile), :] = up[:, :E]
-            den[h, pl.ds(base, tile), :] = up[:, E:]
-            att[h, pl.ds(base + tile, tile), :] = down[:, :E]
-            den[h, pl.ds(base + tile, tile), :] = down[:, E:]
-
-    def forward_state(b):
-        def body(h, sums):
-            sq, pr = sums
-            if b == 0:
-                fetch(3, h).wait()
-            full = pfx[0, h]
-            for a in range(b):
-                full = full + kvb[h, a]
-            hi, lo = split(full[:E])
-            sh[h, b] = jnp.concatenate([hi, lo], axis=1)
-            norm = jnp.transpose(jnp.broadcast_to(full[NORM:NORM + 1], (E, E)))
-            nhi, nlo = split(norm)
-            wide = jnp.concatenate([jnp.concatenate([hi, nhi], axis=1),
-                                    jnp.concatenate([lo, nlo], axis=1)], axis=0)
-            f = fq[h, rows(b), :]
-            both = dot(jnp.concatenate([f, f], axis=1), wide)
-            inv = 1.0 / (den[h, rows(b), :] + both[:, E:])
-            out = (att[h, rows(b), :] + both[:, :E]) * inv
-            den[h, rows(b), :] = inv
-            att[h, rows(b), :] = out
-            w = cv[h, rows(b), :].astype(F32) * gain_ref[pl.ds(h, 1), :]
-            return sq + out * out, pr + w * out
-        zero = jnp.zeros((block, E), F32)
-        sq, pr = lax.fori_loop(0, heads, body, (zero, zero))
-        stat[b, 0:1, :] = jnp.sum(jnp.transpose(sq), axis=0, keepdims=True)
-        stat[b, 1:2, :] = jnp.sum(jnp.transpose(pr), axis=0, keepdims=True)
-
-    def share(b, d):
+            w = jnp.where(keep, dot(f, fk[h, rows(b), :], 1, 1), 0.0).astype(BF16)
+            wts[h, b] = w
+            both = dot(w, jnp.concatenate([vv[h, rows(b), :], ones], axis=1))
+            att[h, rows(b), :] = both[:, :E]
+            den[h, rows(b), :] = both[:, E:]
+
+    def forward_state(j):
+        back_in(0, j).wait_recv()
+        pair = (mine + j, theirs + j)
+        full = []
+        for h in pair:
+            fetch(3, h).wait()
+            full.append(pfx[0, h])
+        for b in range(nblk):
+            sq, pr = acc[0, rows(b), :], acc[1, rows(b), :]
+            for i, h in enumerate(pair):
+                hi, lo = split(full[i][:E])
+                sh[h, b] = jnp.concatenate([hi, lo], axis=1)
+                norm = full[i][NORM:NORM + 1]
+                nrm[h, b] = jnp.broadcast_to(norm, (8, E))
+                nhi, nlo = split(jnp.transpose(jnp.broadcast_to(norm, (E, E))))
+                wide = jnp.concatenate([jnp.concatenate([hi, nhi], axis=1),
+                                        jnp.concatenate([lo, nlo], axis=1)], axis=0)
+                f = fq[h, rows(b), :]
+                both = dot(jnp.concatenate([f, f], axis=1), wide)
+                inv = 1.0 / (den[h, rows(b), :] + both[:, E:])
+                out = (att[h, rows(b), :] + both[:, :E]) * inv
+                den[h, rows(b), :] = inv
+                att[h, rows(b), :] = out
+                sq = sq + out * out
+                pr = pr + cv[h, rows(b), :].astype(F32) * gain_ref[pl.ds(h, 1), :] * out
+                full[i] = full[i] + kvb[h, b]
+            acc[0, rows(b), :] = sq
+            acc[1, rows(b), :] = pr
+
+    def share(d):
         return pltpu.make_async_remote_copy(
-            src_ref=stat.at[b], dst_ref=stat_in.at[b, d - 1],
-            send_sem=ss.at[b, d - 1], recv_sem=rs.at[b, d - 1],
+            src_ref=stat, dst_ref=stat_in.at[d - 1],
+            send_sem=ss.at[d - 1], recv_sem=rs.at[d - 1],
             device_id=zpeer(d), device_id_type=MESH)
 
-    def scales(b):
+    def norms():
+        for b in range(nblk):
+            for i in range(2):
+                stat[i:i + 1, b * block:(b + 1) * block] = jnp.sum(
+                    jnp.transpose(acc[i, rows(b), :]), axis=0, keepdims=True)
         for d in range(1, n_head):
-            share(b, d).wait_recv()
-        total = stat[b]
+            share(d).start()
         for d in range(1, n_head):
-            total = total + stat_in[b, d - 1]
+            share(d).wait_recv()
+        total = stat[...]
+        for d in range(1, n_head):
+            total = total + stat_in[d - 1]
         scale = lax.rsqrt(total[0:1] / width + 1e-06)
         pull = scale * scale * scale * total[1:2] / width
-        scl[b, 0] = jnp.transpose(jnp.broadcast_to(scale, (E, block)))
-        scl[b, 1] = jnp.transpose(jnp.broadcast_to(pull, (E, block)))
-
-    def gradient(b, h):
+        for b in range(nblk):
+            for i, x in enumerate((scale, pull)):
+                x = x[:, b * block:(b + 1) * block]
+                acc[i, rows(b), :] = jnp.transpose(jnp.broadcast_to(x, (E, block)))
+
+    def gradient(h):
         gain = gain_ref[pl.ds(h, 1), :]
-        scale, pull = scl[b, 0], scl[b, 1]
-        out, inv = att[h, rows(b), :], den[h, rows(b), :]
-        sg = scale * gain
-        om[h, rows(b), :] = (out * sg).astype(BF16)
-        d = sg * cv[h, rows(b), :].astype(F32) - out * pull
-        g = (d * inv).astype(BF16)
-        gd = -jnp.sum(d * out, axis=1, keepdims=True) * inv
-        gn[h, rows(b), :] = g
-        den[h, rows(b), :] = gd
-        f = fq[h, rows(b), :]
-        later = dot(f, g, 0, 0)
-        lden = jnp.sum(gd * f.astype(F32), axis=0, keepdims=True)
-        part = jnp.concatenate([later, jnp.broadcast_to(lden, (8, E))], axis=0)
-        rvb[h, b] = part
-        tot[1, h] = tot[1, h] + part if b else part
+        total = jnp.zeros((PAY, E), F32)
+        for b in range(nblk):
+            scale, pull = acc[0, rows(b), :], acc[1, rows(b), :]
+            out, inv = att[h, rows(b), :], den[h, rows(b), :]
+            sg = scale * gain
+            om[h, rows(b), :] = (out * sg).astype(BF16)
+            d = sg * cv[h, rows(b), :].astype(F32) - out * pull
+            g = (d * inv).astype(BF16)
+            gd = -jnp.sum(d * out, axis=1, keepdims=True) * inv
+            gn[h, rows(b), :] = g
+            den[h, rows(b), :] = gd
+            f = fq[h, rows(b), :]
+            later = dot(f, g, 0, 0)
+            lden = jnp.sum(gd * f.astype(F32), axis=0, keepdims=True)
+            part = jnp.concatenate([later, jnp.broadcast_to(lden, (8, E))], axis=0)
+            rvb[h, b] = part
+            total = total + part
+        tot[1, h] = total
 
     def backward_local(h):
         keep = causal()
         for b in range(nblk):
-            base = b * block
             f, k, v, g = fq[h, rows(b), :], fk[h, rows(b), :], vv[h, rows(b), :], gn[h, rows(b), :]
             gd = den[h, rows(b), :]
-            gw = jnp.concatenate([gd] * (tile // E), axis=1)
-            top = jnp.where(keep, dot(g[:tile], v[:tile], 1, 1) + gw[:tile], 0.0).astype(BF16)
-            low = dot(g[tile:], v, 1, 1)
-            left = (low[:, :tile] + gw[tile:]).astype(BF16)
-            right = jnp.where(keep, low[:, tile:] + gw[tile:], 0.0).astype(BF16)
-            norm = pfx[0, h, NORM:NORM + 1, :]
-            for a in range(b):
-                norm = norm + kvb[h, a, NORM:NORM + 1, :]
-            far = dot(jnp.concatenate([g, g], axis=1), sh[h, b], 1, 1) + gd * norm
-            up = dot(top, k[:tile]) + far[:tile]
-            down = dot(jnp.concatenate([left, right], axis=1), k) + far[tile:]
-            sl = slope(qv[h, rows(b), :])
-            oq[h, pl.ds(base, tile), :] = (up * sl[:tile]).astype(BF16)
-            oq[h, pl.ds(base + tile, tile), :] = (down * sl[tile:]).astype(BF16)
-            att[h, pl.ds(base, tile), :] = dot(jnp.concatenate([top, left], axis=0), f, 0, 0)
-            att[h, pl.ds(base + tile, tile), :] = dot(right, f[tile:], 0, 0)
-            first = jnp.concatenate([wts[h, b, 0], wts[h, b, 1]], axis=0)
-            dvp[h, pl.ds(base, tile), :] = dot(first, g, 0, 0)
-            dvp[h, pl.ds(base + tile, tile), :] = dot(wts[h, b, 2], g[tile:], 0, 0)
+            gw = jnp.concatenate([gd] * (block // E), axis=1)
+            m = jnp.where(keep, dot(g, v, 1, 1) + gw, 0.0).astype(BF16)
+            far = dot(jnp.concatenate([g, g], axis=1), sh[h, b], 1, 1) + gd * nrm[h, b, 0:1, :]
+            dq = dot(m, k) + far
+            oq[h, rows(b), :] = (dq * slope(qv[h, rows(b), :])).astype(BF16)
+            att[h, rows(b), :] = dot(m, f, 0, 0)
+            dvp[h, rows(b), :] = dot(wts[h, b], g, 0, 0)
 
     def later_sums(h):
         full = pfx[1, h]
@@ -305,43 +293,43 @@
             chip_total(dirn, j)
         each(half, step)
 
-    def middle(dirn, local, slot):
-        events = sorted((slot(s, j), s, j) for s in range(stages) for j in range(half))
+    def middle(dirn, local, slot, after=None):
+        events = sorted((min(slot(s, j), heads + j), s, j)
+                        for s in range(stages) for j in range(half))
+
+        def happen(h):
+            for at, s, j in events:
+                @pl.when(h == at)
+                def _(s=s, j=j):
+                    hop_on(dirn, s, j)
 
         def step(h):
             local(h)
-            for at, s, j in events:
-                if at < heads:
-                    @pl.when(h == at)
-                    def _(s=s, j=j):
-                        hop_on(dirn, s, j)
+            happen(h)
         each(heads, step)
-        for at, s, j in events:
-            if at >= heads:
-                hop_on(dirn, s, j)
-        arrive(dirn)
+
+        def late(j):
+            happen(heads + j)
+            if after is not None:
+                after(j)
+        each(half, late)
+        if after is None:
+            arrive(dirn)
 
     greeted = len(masks) + n_head - 1
+    acc[...] = jnp.zeros_like(acc)
     sums(0, key_sums, lambda: pl.semaphore_wait(barrier, greeted))
-    middle(0, forward_local, lambda s, j: 1 + (3 * j) // 2 + 4 * s)
     gain_copy.wait()
-    for b in range(nblk):
-        forward_state(b)
-        for d in range(1, n_head):
-            share(b, d).start()
-    for b in range(nblk - 1):
-        scales(b)
-        each(heads, functools.partial(gradient, b))
-    scales(nblk - 1)
-    sums(1, functools.partial(gradient, nblk - 1))
-    middle(1, backward_local, lambda s, j: j + 2 * s)
+    middle(0, forward_local, lambda s, j: 1 + 2 * j + 4 * s, forward_state)
+    norms()
+    sums(1, gradient)
+    middle(1, backward_local, lambda s, j: j + 1 + 3 * s)
     each(heads, later_sums)
 
     drain(0)
     drain(1)
-    for b in range(nblk):
-        for d in range(1, n_head):
-            share(b, d).wait_send()
+    for d in range(1, n_head):
+        share(d).wait_send()
 
 
 def last(dims, om, oq, kv, vv, fk, att, dvp, lat, mixed_hbm, gq_hbm, gk_hbm, gv_hbm,
@@ -398,7 +386,7 @@
         half16,
         half16,
         half16,
-        pltpu.VMEM((heads, nblk, 3, block // 2, block // 2), BF16),
+        pltpu.VMEM((heads, nblk, block, block), BF16),
         full32,
         half16,
         pltpu.VMEM((heads, nblk, PAY, E), F32),
@@ -410,9 +398,10 @@
         pltpu.VMEM((2, stages, half, PAY, E), F32),
         pltpu.VMEM((2, half, PAY, E), F32),
         pltpu.VMEM((2, heads, PAY, E), F32),
-        pltpu.VMEM((nblk, 2, block), F32),
-        pltpu.VMEM((nblk, n_head - 1, 2, block), F32),
-        pltpu.VMEM((nblk, 2, block, E), F32),
+        pltpu.VMEM((2, rows), F32),
+        pltpu.VMEM((n_head - 1, 2, rows), F32),
+        pltpu.VMEM((2, rows, E), F32),
+        pltpu.VMEM((heads, nblk, 8, E), F32),
         pltpu.VMEM((heads, E), F32),
         dma,
         dma((4, heads)),
@@ -422,8 +411,8 @@
         dma((2, stages, half)),
         dma((2, half)),
         dma((2, half)),
-        dma((nblk, n_head - 1)),
-        dma((nblk, n_head - 1)),
+        dma((n_head - 1,)),
+        dma((n_head - 1,)),
     ]
     inside = pl.BlockSpec(memory_space=pltpu.VMEM)
     kept = pl.pallas_call(

time: 53 us -> 47.1 us (0.89)
  Pallas kernels: 51.5 us -> 46.2 us
  local copies, waits for them, and re-layouts: 0.68 us -> 0 us
    pallas_call x1, Pallas kernels: 46.8 us -> 41.7 us  [shards(): pl.pallas_call(functools.partial(kernel, dims), out_shape=held, in_specs=...]
    unnamed x2 -> x0, local copies, waits for them, and re-layouts: 0.68 us -> none
where the time goes in v3:
time: 47.1 us; the launch traced here: 46.9 us
  Pallas kernels  46.2 us (98%)
  between operations  0.64 us (1%)
    pallas_call x1, Pallas kernels, shards(): pl.pallas_call(functools.partial(kernel, dims), out_shape=held, in_specs=...  41.7 us
    pallas_call x1, Pallas kernels, shards(): pl.pallas_call(functools.partial(last, dims), out_shape=(out,) * 4, in_sp...  4.57 us

profile of v3, /device:TPU:0, one launch (start us, length us, event | category | flops | bytes accessed | tf_op | source)
XLA Modules:
  0.0 46.9 jit_solution(10325277221301285739)
XLA Ops:
  0.6 41.7 %shard_map.84 = (bf16[8,1024,128]{2,1,0:T(8,128)(2,1)S(1)}, bf16[8,1024,128]{2,1,0:T(8,128)(2,1)S(1)}, bf16[8,1024,128]{2,1,0:T(8,128)(2,1)S(1)}, bf16[8,1024,12...) custom-call(bf16[1024,1024]{1,0:T(8,128)(2,1)} %q_hbm.1, ...), custom_call_target="tpu_custom_call" | custom-call | flops 4294967296 | bytes 8388608 | tf_op jit(solution)/shard_map/pallas_call | solution.py:418
  42.3 4.6 %shard_map.85 = (bf16[1024,1024]{1,0:T(8,128)(2,1)}, bf16[1024,1024]{1,0:T(8,128)(2,1)}, bf16[1024,1024]{1,0:T(8,128)(2,1)}, bf16[1024,1024]{1,0:T(8,128)(2,1)}) custom-call(bf16[8,1024,128]{2,1,0:T(8,128)(2,1)S(1)} %get-tuple-element.12.om, bf16[8,1024,128]{2,1,0:T(8,128)(2,1)S(1)} %get-tuple-element.13.oq, bf16[8,1024,128]{2,1,0:T(8,128)(2,1)S(1)} %get-tuple-element.14.kv, ...), custom_call_target="tpu_custom_call" | custom-call | flops 1073741824 | bytes 8388608 | tf_op jit(solution)/shard_map/pallas_call | solution.py:433

commit v4 on v3

--- a/solution.py
+++ b/solution.py
@@ -13,7 +13,7 @@
 PAY = E + 8
 F32 = jnp.float32
 BF16 = jnp.bfloat16
-VMEM_A = 34 * 1024 * 1024
+VMEM_A = 48 * 1024 * 1024
 VMEM_B = 8 * 1024 * 1024
 MESH = pl.DeviceIdType.MESH
 
@@ -23,8 +23,8 @@
     return jnp.where(xf > 0, xf + 1.0, jnp.exp(jnp.minimum(xf, 0.0))).astype(BF16)
 
 
-def slope(x):
-    return jnp.exp(jnp.minimum(x.astype(F32), 0.0))
+def slope(f):
+    return jnp.minimum(f.astype(F32), 1.0)
 
 
 def dot(a, b, ca=1, cb=0):
@@ -43,8 +43,8 @@
     lax.fori_loop(0, n, step, 0)
 
 
-def kernel(dims, q_hbm, k_hbm, v_hbm, g_hbm, c_hbm, om, oq, kv, vv, fk, att, dvp, lat,
-           qv, cv, fq, wts, den, gn, kvb, rvb, sh, tot, r0, tx, rx, fin, pfx, stat, stat_in, acc, nrm,
+def kernel(dims, q_hbm, k_hbm, v_hbm, g_hbm, c_hbm, om, oq, ok, ov,
+           qv, kv, vv, cv, fq, fk, att, dvp, wts, den, gn, kvb, rvb, sh, tot, r0, tx, rx, fin, pfx, stat, stat_in, acc, nrm,
            gain_ref, gain_sem, in_sem, s0, q0, sx, rxs, s2, q2, ss, rs):
     heads, nblk, block, n_in, n_out, n_head, width = dims
     half = heads // 2
@@ -137,9 +137,6 @@
         fin[dirn, j] = total + jnp.where(near, own, 0.0)
         pfx[dirn, mine + j] = total + jnp.where(near, 0.0, other)
         back(dirn, j).start()
-
-    def arrive(dirn):
-        each(half, lambda j: back_in(dirn, j).wait_recv())
 
     def drain(dirn):
         def body(j):
@@ -267,15 +264,23 @@
             m = jnp.where(keep, dot(g, v, 1, 1) + gw, 0.0).astype(BF16)
             far = dot(jnp.concatenate([g, g], axis=1), sh[h, b], 1, 1) + gd * nrm[h, b, 0:1, :]
             dq = dot(m, k) + far
-            oq[h, rows(b), :] = (dq * slope(qv[h, rows(b), :])).astype(BF16)
+            oq[h, rows(b), :] = (dq * slope(f)).astype(BF16)
             att[h, rows(b), :] = dot(m, f, 0, 0)
             dvp[h, rows(b), :] = dot(wts[h, b], g, 0, 0)
 
-    def later_sums(h):
-        full = pfx[1, h]
-        for b in reversed(range(nblk)):
-            lat[h, b] = full
-            full = full + rvb[h, b]
+    def backward_state(j):
+        back_in(1, j).wait_recv()
+        for h in (mine + j, theirs + j):
+            full = pfx[1, h]
+            for b in reversed(range(nblk)):
+                hi, lo = split(full[:E])
+                v, k = vv[h, rows(b), :], fk[h, rows(b), :]
+                dk = dot(jnp.concatenate([v, v], axis=1), jnp.concatenate([hi, lo], axis=1), 1, 1)
+                dk = dk + att[h, rows(b), :] + full[NORM:NORM + 1]
+                ok[h, rows(b), :] = (dk * slope(k)).astype(BF16)
+                dv = dot(jnp.concatenate([k, k], axis=1), jnp.concatenate([hi, lo], axis=0))
+                ov[h, rows(b), :] = (dv + dvp[h, rows(b), :]).astype(BF16)
+                full = full + rvb[h, b]
 
     def sums(dirn, body, greet=None):
         body(theirs)
@@ -293,7 +298,7 @@
             chip_total(dirn, j)
         each(half, step)
 
-    def middle(dirn, local, slot, after=None):
+    def middle(dirn, local, slot, after):
         events = sorted((min(slot(s, j), heads + j), s, j)
                         for s in range(stages) for j in range(half))
 
@@ -310,11 +315,8 @@
 
         def late(j):
             happen(heads + j)
-            if after is not None:
-                after(j)
+            after(j)
         each(half, late)
-        if after is None:
-            arrive(dirn)
 
     greeted = len(masks) + n_head - 1
     acc[...] = jnp.zeros_like(acc)
@@ -323,8 +325,7 @@
     middle(0, forward_local, lambda s, j: 1 + 2 * j + 4 * s, forward_state)
     norms()
     sums(1, gradient)
-    middle(1, backward_local, lambda s, j: j + 1 + 3 * s)
-    each(heads, later_sums)
+    middle(1, backward_local, lambda s, j: j + 1 + 3 * s, backward_state)
 
     drain(0)
     drain(1)
@@ -332,39 +333,21 @@
         share(d).wait_send()
 
 
-def last(dims, om, oq, kv, vv, fk, att, dvp, lat, mixed_hbm, gq_hbm, gk_hbm, gv_hbm,
-         ok, ov, out_sem):
-    heads, nblk, block = dims[:3]
-
+def last(heads, om, oq, ok, ov, mixed_hbm, gq_hbm, gk_hbm, gv_hbm, out_sem):
     def put(array, h):
         src, dst = ((om, mixed_hbm), (oq, gq_hbm), (ok, gk_hbm), (ov, gv_hbm))[array]
         cols = pl.ds(pl.multiple_of(h * E, E), E)
         return pltpu.make_async_copy(src.at[h], dst.at[:, cols], out_sem.at[array, h])
 
-    def ready(h):
-        put(0, h).start()
-        put(1, h).start()
-
-    def backward_state(h):
-        for b in range(nblk):
-            rows = pl.ds(b * block, block)
-            full = lat[h, b]
-            hi, lo = split(full[:E])
-            v, k = vv[h, rows, :], fk[h, rows, :]
-            dk = dot(jnp.concatenate([v, v], axis=1), jnp.concatenate([hi, lo], axis=1), 1, 1)
-            dk = dk + att[h, rows, :] + full[NORM:NORM + 1]
-            ok[h, rows, :] = (dk * slope(kv[h, rows, :])).astype(BF16)
-            dv = dot(jnp.concatenate([k, k], axis=1), jnp.concatenate([hi, lo], axis=0))
-            ov[h, rows, :] = (dv + dvp[h, rows, :]).astype(BF16)
-        put(2, h).start()
-        put(3, h).start()
+    def begin(h):
+        for array in range(4):
+            put(array, h).start()
 
     def finish(h):
         for array in range(4):
             put(array, h).wait()
 
-    each(heads, ready)
-    each(heads, backward_state)
+    each(heads, begin)
     each(heads, finish)
 
 
@@ -381,11 +364,10 @@
     anywhere = pl.BlockSpec(memory_space=pl.ANY)
     dma = pltpu.SemaphoreType.DMA
     half16, full32 = pltpu.VMEM(whole, BF16), pltpu.VMEM(whole, F32)
-    held = (half16,) * 5 + (full32,) * 2 + (pltpu.VMEM((heads, nblk, PAY, E), F32),)
-    scratch = [
-        half16,
-        half16,
-        half16,
+    held = (half16,) * 4
+    scratch = [half16] * 6 + [
+        full32,
+        full32,
         pltpu.VMEM((heads, nblk, block, block), BF16),
         full32,
         half16,
@@ -431,15 +413,14 @@
     )(queries, keys, values, gain.reshape(heads, E), cotangent)
     out = jax.ShapeDtypeStruct((rows, width), BF16)
     return pl.pallas_call(
-        functools.partial(last, dims),
+        functools.partial(last, heads),
         out_shape=(out,) * 4,
         in_specs=[inside] * len(held),
         out_specs=(anywhere,) * 4,
-        scratch_shapes=[half16, half16, dma((4, heads))],
+        scratch_shapes=[dma((4, heads))],
         compiler_params=pltpu.CompilerParams(vmem_limit_bytes=VMEM_B),
         cost_estimate=pl.CostEstimate(
-            flops=4 * rows * 2 * E * width, bytes_accessed=8 * rows * width,
-            transcendentals=rows * width,
+            flops=0, bytes_accessed=8 * rows * width, transcendentals=0,
         ),
     )(*kept)
 

time: 47.1 us -> 48.1 us (1.021)
  Pallas kernels: 46.2 us -> 47.3 us
    pallas_call x1, Pallas kernels: 41.7 us -> 43.7 us  [shards(): pl.pallas_call(functools.partial(kernel, dims), out_shape=held, in_specs=...]
    pallas_call x1, Pallas kernels: 4.57 us -> 3.54 us  [shards(): pl.pallas_call(functools.partial(last, heads), out_shape=(out,) * 4, in_s...]
where the time goes in v4:
time: 48.1 us; the launch traced here: 47.9 us
  Pallas kernels  47.3 us (98%)
  between operations  0.64 us (1%)
    pallas_call x1, Pallas kernels, shards(): pl.pallas_call(functools.partial(kernel, dims), out_shape=held, in_specs=...  43.7 us
    pallas_call x1, Pallas kernels, shards(): pl.pallas_call(functools.partial(last, heads), out_shape=(out,) * 4, in_s...  3.54 us

profile of v4, /device:TPU:0, one launch (start us, length us, event | category | flops | bytes accessed | tf_op | source)
XLA Modules:
  0.0 47.9 jit_solution(15015638280717899154)
XLA Ops:
  0.6 43.7 %shard_map.84 = (bf16[8,1024,128]{2,1,0:T(8,128)(2,1)S(1)}, bf16[8,1024,128]{2,1,0:T(8,128)(2,1)S(1)}, bf16[8,1024,128]{2,1,0:T(8,128)(2,1)S(1)}, bf16[8,1024,128]{2,1,0:T(8,128)(2,1)S(1)}) custom-call(bf16[1024,1024]{1,0:T(8,128)(2,1)} %q_hbm.1, bf16[1024,1024]{1,0:T(8,128)(2,1)} %k_hbm.1, bf16[1024,1024]{1,0:T(8,128)(2,1)} %v_hbm.1, f32[8,128]{1,0:T(8,128)} %bitcast.1, ...), custom_call_target="tpu_custom_call" | custom-call | flops 4294967296 | bytes 8388608 | tf_op jit(solution)/shard_map/pallas_call | solution.py:400
  44.4 3.5 %shard_map.85 = (bf16[1024,1024]{1,0:T(8,128)(2,1)}, bf16[1024,1024]{1,0:T(8,128)(2,1)}, bf16[1024,1024]{1,0:T(8,128)(2,1)}, bf16[1024,1024]{1,0:T(8,128)(2,1)}) custom-call(bf16[8,1024,128]{2,1,0:T(8,128)(2,1)S(1)} %get-tuple-element.8.om, bf16[8,1024,128]{2,1,0:T(8,128)(2,1)S(1)} %get-tuple-element.9.oq, bf16[8,1024,128]{2,1,0:T(8,128)(2,1)S(1)} %get-tuple-element.10.ok, ...), custom_call_target="tpu_custom_call" | custom-call | bytes 8388608 | tf_op jit(solution)/shard_map/pallas_call | solution.py:415

commit v5 on v3

--- a/solution.py
+++ b/solution.py
@@ -13,7 +13,7 @@
 PAY = E + 8
 F32 = jnp.float32
 BF16 = jnp.bfloat16
-VMEM_A = 34 * 1024 * 1024
+VMEM_A = 40 * 1024 * 1024
 VMEM_B = 8 * 1024 * 1024
 MESH = pl.DeviceIdType.MESH
 
@@ -23,8 +23,13 @@
     return jnp.where(xf > 0, xf + 1.0, jnp.exp(jnp.minimum(xf, 0.0))).astype(BF16)
 
 
-def slope(x):
-    return jnp.exp(jnp.minimum(x.astype(F32), 0.0))
+def slope(f):
+    return jnp.minimum(f.astype(F32), 1.0)
+
+
+def inverse(x):
+    r = pl.reciprocal(x, approx=True)
+    return r * (2.0 - x * r)
 
 
 def dot(a, b, ca=1, cb=0):
@@ -43,8 +48,8 @@
     lax.fori_loop(0, n, step, 0)
 
 
-def kernel(dims, q_hbm, k_hbm, v_hbm, g_hbm, c_hbm, om, oq, kv, vv, fk, att, dvp, lat,
-           qv, cv, fq, wts, den, gn, kvb, rvb, sh, tot, r0, tx, rx, fin, pfx, stat, stat_in, acc, nrm,
+def kernel(dims, q_hbm, k_hbm, v_hbm, g_hbm, c_hbm, om, oq, vv, fk, att, dvp, lat,
+           qv, kv, cv, fq, wts, den, gn, kvb, rvb, sh, tot, r0, tx, rx, fin, pfx, stat, stat_in, acc, nrm, mask, gdp,
            gain_ref, gain_sem, in_sem, s0, q0, sx, rxs, s2, q2, ss, rs):
     heads, nblk, block, n_in, n_out, n_head, width = dims
     half = heads // 2
@@ -167,18 +172,20 @@
         tot[0, h] = total
 
     def causal():
-        return (lax.broadcasted_iota(jnp.int32, (block, block), 0)
-                >= lax.broadcasted_iota(jnp.int32, (block, block), 1))
+        t = lax.broadcasted_iota(jnp.int32, (block, block), 0)
+        u = lax.broadcasted_iota(jnp.int32, (block, block), 1)
+        mask[0] = jnp.where(t >= u, 1.0, 0.0).astype(BF16)
+        mask[1] = jnp.where(t <= u, 1.0, 0.0).astype(BF16)
 
     def forward_local(h):
         fetch(2, h).wait()
-        keep = causal()
         ones = jnp.ones((block, E), BF16)
         for b in range(nblk):
             f = features(qv[h, rows(b), :])
             fq[h, rows(b), :] = f
-            w = jnp.where(keep, dot(f, fk[h, rows(b), :], 1, 1), 0.0).astype(BF16)
-            wts[h, b] = w
+            k = fk[h, rows(b), :]
+            w = dot(f, k, 1, 1).astype(BF16) * mask[0]
+            wts[h, b] = dot(k, f, 1, 1).astype(BF16) * mask[1]
             both = dot(w, jnp.concatenate([vv[h, rows(b), :], ones], axis=1))
             att[h, rows(b), :] = both[:, :E]
             den[h, rows(b), :] = both[:, E:]
@@ -202,7 +209,7 @@
                                         jnp.concatenate([lo, nlo], axis=1)], axis=0)
                 f = fq[h, rows(b), :]
                 both = dot(jnp.concatenate([f, f], axis=1), wide)
-                inv = 1.0 / (den[h, rows(b), :] + both[:, E:])
+                inv = inverse(den[h, rows(b), :] + both[:, E:])
                 out = (att[h, rows(b), :] + both[:, :E]) * inv
                 den[h, rows(b), :] = inv
                 att[h, rows(b), :] = out
@@ -240,6 +247,7 @@
     def gradient(h):
         gain = gain_ref[pl.ds(h, 1), :]
         total = jnp.zeros((PAY, E), F32)
+        lane = lax.broadcasted_iota(jnp.int32, (block, E), 1)
         for b in range(nblk):
             scale, pull = acc[0, rows(b), :], acc[1, rows(b), :]
             out, inv = att[h, rows(b), :], den[h, rows(b), :]
@@ -250,6 +258,8 @@
             gd = -jnp.sum(d * out, axis=1, keepdims=True) * inv
             gn[h, rows(b), :] = g
             den[h, rows(b), :] = gd
+            rest = gd - gd.astype(BF16).astype(F32)
+            gdp[h, rows(b), :] = jnp.where(lane == 0, gd, jnp.where(lane == 1, rest, 0.0)).astype(BF16)
             f = fq[h, rows(b), :]
             later = dot(f, g, 0, 0)
             lden = jnp.sum(gd * f.astype(F32), axis=0, keepdims=True)
@@ -259,17 +269,19 @@
         tot[1, h] = total
 
     def backward_local(h):
-        keep = causal()
+        ones = jnp.ones((block, E), BF16)
         for b in range(nblk):
             f, k, v, g = fq[h, rows(b), :], fk[h, rows(b), :], vv[h, rows(b), :], gn[h, rows(b), :]
-            gd = den[h, rows(b), :]
-            gw = jnp.concatenate([gd] * (block // E), axis=1)
-            m = jnp.where(keep, dot(g, v, 1, 1) + gw, 0.0).astype(BF16)
-            far = dot(jnp.concatenate([g, g], axis=1), sh[h, b], 1, 1) + gd * nrm[h, b, 0:1, :]
+            va = jnp.concatenate([v, ones], axis=1)
+            ga = jnp.concatenate([g, gdp[h, rows(b), :]], axis=1)
+            m = dot(ga, va, 1, 1).astype(BF16) * mask[0]
+            mt = dot(va, ga, 1, 1).astype(BF16) * mask[1]
+            far = dot(jnp.concatenate([g, g], axis=1), sh[h, b], 1, 1)
+            far = far + den[h, rows(b), :] * nrm[h, b, 0:1, :]
             dq = dot(m, k) + far
-            oq[h, rows(b), :] = (dq * slope(qv[h, rows(b), :])).astype(BF16)
-            att[h, rows(b), :] = dot(m, f, 0, 0)
-            dvp[h, rows(b), :] = dot(wts[h, b], g, 0, 0)
+            oq[h, rows(b), :] = (dq * slope(f)).astype(BF16)
+            att[h, rows(b), :] = dot(mt, f)
+            dvp[h, rows(b), :] = dot(wts[h, b], g)
 
     def later_sums(h):
         full = pfx[1, h]
@@ -318,6 +330,7 @@
 
     greeted = len(masks) + n_head - 1
     acc[...] = jnp.zeros_like(acc)
+    causal()
     sums(0, key_sums, lambda: pl.semaphore_wait(barrier, greeted))
     gain_copy.wait()
     middle(0, forward_local, lambda s, j: 1 + 2 * j + 4 * s, forward_state)
@@ -332,7 +345,7 @@
         share(d).wait_send()
 
 
-def last(dims, om, oq, kv, vv, fk, att, dvp, lat, mixed_hbm, gq_hbm, gk_hbm, gv_hbm,
+def last(dims, om, oq, vv, fk, att, dvp, lat, mixed_hbm, gq_hbm, gk_hbm, gv_hbm,
          ok, ov, out_sem):
     heads, nblk, block = dims[:3]
 
@@ -353,7 +366,7 @@
             v, k = vv[h, rows, :], fk[h, rows, :]
             dk = dot(jnp.concatenate([v, v], axis=1), jnp.concatenate([hi, lo], axis=1), 1, 1)
             dk = dk + att[h, rows, :] + full[NORM:NORM + 1]
-            ok[h, rows, :] = (dk * slope(kv[h, rows, :])).astype(BF16)
+            ok[h, rows, :] = (dk * slope(k)).astype(BF16)
             dv = dot(jnp.concatenate([k, k], axis=1), jnp.concatenate([hi, lo], axis=0))
             ov[h, rows, :] = (dv + dvp[h, rows, :]).astype(BF16)
         put(2, h).start()
@@ -381,11 +394,8 @@
     anywhere = pl.BlockSpec(memory_space=pl.ANY)
     dma = pltpu.SemaphoreType.DMA
     half16, full32 = pltpu.VMEM(whole, BF16), pltpu.VMEM(whole, F32)
-    held = (half16,) * 5 + (full32,) * 2 + (pltpu.VMEM((heads, nblk, PAY, E), F32),)
-    scratch = [
-        half16,
-        half16,
-        half16,
+    held = (half16,) * 4 + (full32,) * 2 + (pltpu.VMEM((heads, nblk, PAY, E), F32),)
+    scratch = [half16] * 4 + [
         pltpu.VMEM((heads, nblk, block, block), BF16),
         full32,
         half16,
@@ -402,6 +412,8 @@
         pltpu.VMEM((n_head - 1, 2, rows), F32),
         pltpu.VMEM((2, rows, E), F32),
         pltpu.VMEM((heads, nblk, 8, E), F32),
+        pltpu.VMEM((2, block, block), BF16),
+        half16,
         pltpu.VMEM((heads, E), F32),
         dma,
         dma((4, heads)),

time: 47.1 us -> 46.2 us (0.981)
  Pallas kernels: 46.2 us -> 45.3 us
    pallas_call x1, Pallas kernels: 41.7 us -> 40.7 us  [shards(): pl.pallas_call(functools.partial(kernel, dims), out_shape=held, in_specs=...]
where the time goes in v5:
time: 46.2 us; the launch traced here: 45.9 us
  Pallas kernels  45.3 us (98%)
  between operations  0.64 us (1%)
    pallas_call x1, Pallas kernels, shards(): pl.pallas_call(functools.partial(kernel, dims), out_shape=held, in_specs=...  40.7 us
    pallas_call x1, Pallas kernels, shards(): pl.pallas_call(functools.partial(last, dims), out_shape=(out,) * 4, in_sp...  4.58 us

profile of v5, /device:TPU:0, one launch (start us, length us, event | category | flops | bytes accessed | tf_op | source)
XLA Modules:
  0.0 45.9 jit_solution(5124162022480783968)
XLA Ops:
  0.6 40.7 %shard_map.84 = (bf16[8,1024,128]{2,1,0:T(8,128)(2,1)S(1)}, bf16[8,1024,128]{2,1,0:T(8,128)(2,1)S(1)}, bf16[8,1024,128]{2,1,0:T(8,128)(2,1)S(1)}, bf16[8,1024,12...) custom-call(bf16[1024,1024]{1,0:T(8,128)(2,1)} %q_hbm.1, ...), custom_call_target="tpu_custom_call" | custom-call | flops 4294967296 | bytes 8388608 | tf_op jit(solution)/shard_map/pallas_call | solution.py:430
  41.3 4.6 %shard_map.85 = (bf16[1024,1024]{1,0:T(8,128)(2,1)}, bf16[1024,1024]{1,0:T(8,128)(2,1)}, bf16[1024,1024]{1,0:T(8,128)(2,1)}, bf16[1024,1024]{1,0:T(8,128)(2,1)}) custom-call(bf16[8,1024,128]{2,1,0:T(8,128)(2,1)S(1)} %get-tuple-element.11.om, bf16[8,1024,128]{2,1,0:T(8,128)(2,1)S(1)} %get-tuple-element.12.oq, bf16[8,1024,128]{2,1,0:T(8,128)(2,1)S(1)} %get-tuple-element.13.vv, ...), custom_call_target="tpu_custom_call" | custom-call | flops 1073741824 | bytes 8388608 | tf_op jit(solution)/shard_map/pallas_call | solution.py:445

commit v6 on v5

--- a/solution.py
+++ b/solution.py
@@ -69,6 +69,16 @@
         other = me + m - 2 * m * bit(m)
         return (lax.div(other, n_out), lax.rem(other, n_out), a_head)
 
+    cross = stages == 2
+
+    def hop_peer(s):
+        a = 2 << s
+        b = 2 << (stages - 1 - s) if cross else a
+        m = a + core * (b - a)
+        at = bit(a) + core * (bit(b) - bit(a))
+        other = me + m - 2 * m * at
+        return (lax.div(other, n_out), lax.rem(other, n_out), a_head)
+
     def zpeer(d):
         return (a_in, a_out, lax.rem(a_head + d, n_head))
 
@@ -108,7 +118,7 @@
         return pltpu.make_async_remote_copy(
             src_ref=tx.at[dirn, s, j], dst_ref=rx.at[dirn, s, j],
             send_sem=sx.at[dirn, s, j], recv_sem=rxs.at[dirn, s, j],
-            device_id=peer(2 << s), device_id_type=MESH)
+            device_id=hop_peer(s), device_id_type=MESH)
 
     def back(dirn, j):
         return pltpu.make_async_remote_copy(
@@ -130,12 +140,20 @@
     def hop_on(dirn, s, j):
         hop(dirn, s, j).wait_recv()
         if s + 1 < stages:
-            tx[dirn, s + 1, j] = tx[dirn, s, j] + rx[dirn, s, j]
+            own, got = tx[dirn, s, j], rx[dirn, s, j]
+            if cross:
+                own = jnp.where(jnp.logical_or(core == 0, bit(2) == dirn), own, 0.0)
+                got = jnp.where(jnp.logical_or(core == 0, bit(4) == 1 - dirn), got, 0.0)
+            tx[dirn, s + 1, j] = own + got
             hop(dirn, s + 1, j).start()
             return
         total = jnp.zeros((PAY, E), F32)
         for i in range(stages):
             before = bit(2 << i) == 1 - dirn
+            if cross:
+                turned = (bit(4) == 1 - dirn) if i == 0 else (core == 1)
+                before = jnp.logical_or(jnp.logical_and(core == 0, before),
+                                        jnp.logical_and(core == 1, turned))
             total = total + jnp.where(before, rx[dirn, i, j], 0.0)
         near = core == dirn
         own, other = tot[dirn, mine + j], r0[dirn, j]
@@ -306,7 +324,7 @@
         each(half, step)
 
     def middle(dirn, local, slot, after=None):
-        events = sorted((min(slot(s, j), heads + j), s, j)
+        events = sorted((min(slot(s, j), heads + j - 1), s, j)
                         for s in range(stages) for j in range(half))
 
         def happen(h):
@@ -321,9 +339,9 @@
         each(heads, step)
 
         def late(j):
-            happen(heads + j)
             if after is not None:
                 after(j)
+            happen(heads + j)
         each(half, late)
         if after is None:
             arrive(dirn)
@@ -336,7 +354,7 @@
     middle(0, forward_local, lambda s, j: 1 + 2 * j + 4 * s, forward_state)
     norms()
     sums(1, gradient)
-    middle(1, backward_local, lambda s, j: j + 1 + 3 * s)
+    middle(1, backward_local, lambda s, j: j + 3 * s)
     each(heads, later_sums)
 
     drain(0)

time: 46.2 us -> 45.1 us (0.976)
  Pallas kernels: 45.3 us -> 44.3 us
    pallas_call x1, Pallas kernels: 40.7 us -> 39.8 us  [shards(): pl.pallas_call(functools.partial(kernel, dims), out_shape=held, in_specs=...]
where the time goes in v6:
time: 45.1 us; the launch traced here: 45 us
  Pallas kernels  44.3 us (98%)
  between operations  0.64 us (1%)
    pallas_call x1, Pallas kernels, shards(): pl.pallas_call(functools.partial(kernel, dims), out_shape=held, in_specs=...  39.8 us
    pallas_call x1, Pallas kernels, shards(): pl.pallas_call(functools.partial(last, dims), out_shape=(out,) * 4, in_sp...  4.58 us

profile of v6, /device:TPU:0, one launch (start us, length us, event | category | flops | bytes accessed | tf_op | source)
XLA Modules:
  0.0 45.0 jit_solution(7009383906707259720)
XLA Ops:
  0.6 39.8 %shard_map.84 = (bf16[8,1024,128]{2,1,0:T(8,128)(2,1)S(1)}, bf16[8,1024,128]{2,1,0:T(8,128)(2,1)S(1)}, bf16[8,1024,128]{2,1,0:T(8,128)(2,1)S(1)}, bf16[8,1024,12...) custom-call(bf16[1024,1024]{1,0:T(8,128)(2,1)} %q_hbm.1, ...), custom_call_target="tpu_custom_call" | custom-call | flops 4294967296 | bytes 8388608 | tf_op jit(solution)/shard_map/pallas_call | solution.py:448
  40.4 4.6 %shard_map.85 = (bf16[1024,1024]{1,0:T(8,128)(2,1)}, bf16[1024,1024]{1,0:T(8,128)(2,1)}, bf16[1024,1024]{1,0:T(8,128)(2,1)}, bf16[1024,1024]{1,0:T(8,128)(2,1)}) custom-call(bf16[8,1024,128]{2,1,0:T(8,128)(2,1)S(1)} %get-tuple-element.11.om, bf16[8,1024,128]{2,1,0:T(8,128)(2,1)S(1)} %get-tuple-element.12.oq, bf16[8,1024,128]{2,1,0:T(8,128)(2,1)S(1)} %get-tuple-element.13.vv, ...), custom_call_target="tpu_custom_call" | custom-call | flops 1073741824 | bytes 8388608 | tf_op jit(solution)/shard_map/pallas_call | solution.py:463

commit v7 on v6

--- a/solution.py
+++ b/solution.py
@@ -351,7 +351,7 @@
     causal()
     sums(0, key_sums, lambda: pl.semaphore_wait(barrier, greeted))
     gain_copy.wait()
-    middle(0, forward_local, lambda s, j: 1 + 2 * j + 4 * s, forward_state)
+    middle(0, forward_local, lambda s, j: 1 + j + 4 * s, forward_state)
     norms()
     sums(1, gradient)
     middle(1, backward_local, lambda s, j: j + 3 * s)

time: 45.1 us -> 43.2 us (0.958)
  Pallas kernels: 44.3 us -> 42.4 us
    pallas_call x1, Pallas kernels: 39.8 us -> 37.8 us  [shards(): pl.pallas_call(functools.partial(kernel, dims), out_shape=held, in_specs=...]
where the time goes in v7:
time: 43.2 us; the launch traced here: 43.1 us
  Pallas kernels  42.4 us (98%)
  between operations  0.64 us (1%)
    pallas_call x1, Pallas kernels, shards(): pl.pallas_call(functools.partial(kernel, dims), out_shape=held, in_specs=...  37.8 us
    pallas_call x1, Pallas kernels, shards(): pl.pallas_call(functools.partial(last, dims), out_shape=(out,) * 4, in_sp...  4.58 us

profile of v7, /device:TPU:0, one launch (start us, length us, event | category | flops | bytes accessed | tf_op | source)
XLA Modules:
  0.0 43.1 jit_solution(5771608417251893440)
XLA Ops:
  0.6 37.8 %shard_map.84 = (bf16[8,1024,128]{2,1,0:T(8,128)(2,1)S(1)}, bf16[8,1024,128]{2,1,0:T(8,128)(2,1)S(1)}, bf16[8,1024,128]{2,1,0:T(8,128)(2,1)S(1)}, bf16[8,1024,12...) custom-call(bf16[1024,1024]{1,0:T(8,128)(2,1)} %q_hbm.1, ...), custom_call_target="tpu_custom_call" | custom-call | flops 4294967296 | bytes 8388608 | tf_op jit(solution)/shard_map/pallas_call | solution.py:448
  38.5 4.6 %shard_map.85 = (bf16[1024,1024]{1,0:T(8,128)(2,1)}, bf16[1024,1024]{1,0:T(8,128)(2,1)}, bf16[1024,1024]{1,0:T(8,128)(2,1)}, bf16[1024,1024]{1,0:T(8,128)(2,1)}) custom-call(bf16[8,1024,128]{2,1,0:T(8,128)(2,1)S(1)} %get-tuple-element.11.om, bf16[8,1024,128]{2,1,0:T(8,128)(2,1)S(1)} %get-tuple-element.12.oq, bf16[8,1024,128]{2,1,0:T(8,128)(2,1)S(1)} %get-tuple-element.13.vv, ...), custom_call_target="tpu_custom_call" | custom-call | flops 1073741824 | bytes 8388608 | tf_op jit(solution)/shard_map/pallas_call | solution.py:463
